TPU v7x, 128 devices: a whole 4x4x4 slice. The times are simulated.
128 devices in a mesh: clip: 4 (over x_hi, core), ctx: 32 (over y, z, x_lo).
Axes of the slice: x: 4 (x_hi: 2, x_lo: 2; x = x_hi * 2 + x_lo), y: 4, z: 4, core: 2. Of those that a mesh axis runs over, the one named last changes fastest.
Arguments:
- queries: bfloat16 [32768, 4096], P(('clip', 'ctx')), parts along dimension 0, may hold values from -128 to 128
- keys: bfloat16 [32768, 4096], P(('clip', 'ctx')), parts along dimension 0, may hold values from -8 to 8
- values: bfloat16 [32768, 4096], P(('clip', 'ctx')), parts along dimension 0, may hold values from -6 to 6
- features: bfloat16 [256, 128, 384], P(('clip', 'ctx')), parts along dimension 0, may hold values from -6 to 6
- feat_grad: bfloat16 [256, 128, 384], P(('clip', 'ctx')), parts along dimension 0, may hold values from -6 to 6
- conv_weight: bfloat16 [3, 384, 384], replicated, may hold values from -0.1875 to 0.1875
- head_weight: bfloat16 [4096, 384], replicated, may hold values from -0.3125 to 0.3125
- pattern: int32 [256, 8], P('clip'), parts along dimension 0, may hold values from 0 to 63, as said below
- live_blocks: int32 [256], P('clip'), parts along dimension 0, may hold values from 1 to 8, as said below
Outputs:
- grad_queries: bfloat16 [32768, 4096], P(('clip', 'ctx')), parts along dimension 0
- grad_keys: bfloat16 [32768, 4096], P(('clip', 'ctx')), parts along dimension 0
- grad_values: bfloat16 [32768, 4096], P(('clip', 'ctx')), parts along dimension 0
- conv_weight_grad: float32 [12, 384, 384], P('clip'), parts along dimension 0
There are 4 independent parts, one for each index of `clip`. A program takes and returns all parts, laid end to end along the dimension named above; an argument that names none is the same for every part. Nothing has to cross between parts.
Inputs may be any that keep to these rules, and one draw needn't show every extreme that they name: `pattern`: row i lists 8 different blocks; its first entry is block i, and the blocks at tile distance 1 to 3 either way, counted cyclically modulo 64, come before others. `live_blocks`: tile 0 has all 8 blocks live.
All inputs are finite; a program needn't handle non-finite values.
Results may differ from a plain program's by a relative error of at most 0.03.
Values may be sent and summed in bfloat16 or wider, within the bound.
No kernel may reach another device: no remote copies, remote signals or barrier semaphores. Data moves between devices by JAX's collectives and lax.ppermute only.
A program may use at most 128 MiB of HBM per device.

v0:
```python
import functools
import math

import jax
import jax.numpy as jnp
from jax import lax
from jax.experimental import pallas as pl
from jax.experimental.pallas import tpu as pltpu
from jax.sharding import PartitionSpec as P

DH = 128
BLK = 128
TOGETHER = 4
GROUP = 8
PACKED = 4
NT = (((1,), (1,)), ((), ()))
TN = (((0,), (0,)), ((), ()))
F32 = jnp.float32
BF16 = jnp.bfloat16
KERNEL_LIMIT = 56 * 1024 * 1024
SMALL_LIMIT = 16 * 1024 * 1024
HBM_SPEC = pl.BlockSpec(memory_space=pl.ANY)
VMEM_SPEC = pl.BlockSpec(memory_space=pltpu.VMEM)


def rows_of(tile):
    return tile >> 1, pl.ds(pl.multiple_of((tile & 1) * BLK, BLK), BLK)


def by_count(count, most, body):
    for size in range(1, most + 1):
        pl.when(count == size)(functools.partial(body, size))


def order_by_count(live_blocks):
    tiles = live_blocks.shape[0]
    ids = jnp.arange(tiles, dtype=jnp.int32)
    here, there = live_blocks[:, None], live_blocks[None, :]
    ahead = (there > here) | ((there == here) & (ids[None, :] < ids[:, None]))
    rank = jnp.sum(ahead.astype(jnp.int32), axis=1)
    placed = (rank[None, :] == ids[:, None]).astype(jnp.int32)
    return jnp.sum(placed * ids[None, :], axis=1)


def columns_of(ref, head):
    return ref.at[:, pl.ds(head * DH, DH)]


def relay(stages):
    for arrivals, _ in stages:
        for copy in arrivals:
            copy.start()
    for arrivals, departures in stages:
        for copy in arrivals:
            copy.wait()
        for copy in departures:
            copy.start()
    for _, departures in stages:
        for copy in departures:
            copy.wait()


def pack_kernel(array_ref, *refs):
    *tap_refs, out_ref, held_ref, in_sems, out_sems = refs
    rows = array_ref.shape[0]
    stages = []
    for first in range(0, out_ref.shape[0], PACKED):
        heads = pl.ds(first, PACKED)
        arrivals = [
            pltpu.make_async_copy(
                columns_of(array_ref, head), held_ref.at[head, pl.ds(0, rows), :], in_sems.at[head]
            )
            for head in range(first, first + PACKED)
        ]
        for tap_ref in tap_refs:
            arrivals.append(
                pltpu.make_async_copy(
                    tap_ref.at[heads],
                    held_ref.at[heads, pl.ds(rows, tap_ref.shape[1]), :],
                    in_sems.at[out_ref.shape[0] + first // PACKED],
                )
            )
        leaving = pltpu.make_async_copy(
            held_ref.at[heads], out_ref.at[heads], out_sems.at[first // PACKED]
        )
        stages.append((arrivals, [leaving]))
    relay(stages)


def pack(array, *taps):
    rows, width = array.shape
    heads = width // DH
    shape = (heads, rows + sum(tap.shape[1] for tap in taps), DH)
    return pl.pallas_call(
        pack_kernel,
        in_specs=[HBM_SPEC] * (1 + len(taps)),
        out_specs=HBM_SPEC,
        out_shape=jax.ShapeDtypeStruct(shape, array.dtype),
        scratch_shapes=[
            pltpu.VMEM(shape, array.dtype),
            pltpu.SemaphoreType.DMA((heads + heads // PACKED,)),
            pltpu.SemaphoreType.DMA((heads // PACKED,)),
        ],
        compiler_params=pltpu.CompilerParams(vmem_limit_bytes=SMALL_LIMIT),
        cost_estimate=pl.CostEstimate(flops=0, bytes_accessed=4 * rows * width, transcendentals=0),
    )(array, *taps)


def share_sum_kernel(terms_ref, into_ref, out_ref, terms, total, in_sem, out_sems):
    held = total.shape[0]
    rows = out_ref.shape[1] - held
    arrival = pltpu.make_async_copy(terms_ref.at[:, pl.ds(rows, held), :], terms, in_sem)
    arrival.start()
    arrival.wait()
    total[...] = jnp.sum(terms[...].astype(F32), axis=0).astype(BF16)
    copies = [
        pltpu.make_async_copy(total, out_ref.at[device, pl.ds(rows, held), :], out_sems.at[device])
        for device in range(out_ref.shape[0])
    ]
    for copy in copies:
        copy.start()
    for copy in copies:
        copy.wait()


def share_sum(terms, into, held):
    devices = terms.shape[0]
    return pl.pallas_call(
        share_sum_kernel,
        in_specs=[HBM_SPEC] * 2,
        out_specs=HBM_SPEC,
        out_shape=jax.ShapeDtypeStruct(into.shape, into.dtype),
        scratch_shapes=[
            pltpu.VMEM((devices, held, DH), BF16),
            pltpu.VMEM((held, DH), BF16),
            pltpu.SemaphoreType.DMA(()),
            pltpu.SemaphoreType.DMA((devices,)),
        ],
        input_output_aliases={1: 0},
        compiler_params=pltpu.CompilerParams(vmem_limit_bytes=SMALL_LIMIT),
    )(terms, into)


def pack_project_kernel(key_ref, grad_ref, weight_ref, out_ref, sems):
    heads, rows = out_ref.shape[0], key_ref.shape[0]
    copies = [
        pltpu.make_async_copy(
            columns_of(key_ref, head), out_ref.at[head, pl.ds(0, rows), :], sems.at[head]
        )
        for head in range(heads)
    ]
    for copy in copies:
        copy.start()
    for head in range(0, heads, 2):
        projected = lax.dot_general(
            grad_ref[...], weight_ref[head * DH : (head + 2) * DH, :], NT, preferred_element_type=F32
        ).astype(BF16)
        out_ref[head, rows:, :] = projected[:, :DH]
        out_ref[head + 1, rows:, :] = projected[:, DH:]
    for copy in copies:
        copy.wait()


def pack_project(keys, feature_grad, head_weight):
    rows, width = keys.shape
    heads = width // DH
    channels = feature_grad.shape[1]
    return pl.pallas_call(
        pack_project_kernel,
        in_specs=[HBM_SPEC, VMEM_SPEC, VMEM_SPEC],
        out_specs=VMEM_SPEC,
        out_shape=jax.ShapeDtypeStruct((heads, 2 * rows, DH), keys.dtype),
        scratch_shapes=[pltpu.SemaphoreType.DMA((heads,))],
        compiler_params=pltpu.CompilerParams(vmem_limit_bytes=KERNEL_LIMIT),
        cost_estimate=pl.CostEstimate(
            flops=2 * rows * width * channels, bytes_accessed=8 * rows * width, transcendentals=0
        ),
    )(keys, feature_grad, head_weight)


def unpack_kernel(pair_ref, last_ref, *refs):
    *out_refs, held_ref, in_sems, out_sems = refs
    heads, rows = held_ref.shape[0], out_refs[0].shape[0]
    stages = []
    for first in range(0, heads, PACKED):
        group = pl.ds(first, PACKED)
        places = [(pair_ref, 0, 2 * rows), (last_ref, 2 * rows, rows)]
        arrivals = [
            pltpu.make_async_copy(
                ref.at[group, pl.ds(0, length), :],
                held_ref.at[group, pl.ds(start, length), :],
                in_sems.at[place, first // PACKED],
            )
            for place, (ref, start, length) in enumerate(places)
        ]
        departures = [
            pltpu.make_async_copy(
                held_ref.at[head, pl.ds(place * rows, rows), :],
                columns_of(out_ref, head),
                out_sems.at[place, head],
            )
            for head in range(first, first + PACKED)
            for place, out_ref in enumerate(out_refs)
        ]
        stages.append((arrivals, departures))
    relay(stages)


def unpack(pair, last):
    heads, rows = pair.shape[0], pair.shape[1] // 2
    return pl.pallas_call(
        unpack_kernel,
        in_specs=[HBM_SPEC] * 2,
        out_specs=[HBM_SPEC] * 3,
        out_shape=[jax.ShapeDtypeStruct((rows, heads * DH), last.dtype)] * 3,
        scratch_shapes=[
            pltpu.VMEM((heads, 3 * rows, DH), last.dtype),
            pltpu.SemaphoreType.DMA((2, heads // PACKED)),
            pltpu.SemaphoreType.DMA((3, heads)),
        ],
        compiler_params=pltpu.CompilerParams(vmem_limit_bytes=SMALL_LIMIT),
        cost_estimate=pl.CostEstimate(
            flops=0, bytes_accessed=12 * rows * heads * DH, transcendentals=0
        ),
    )(pair, last)


def clear(total_ref):
    def step(block, carry):
        total_ref[block] = jnp.zeros(total_ref.shape[1:], F32)
        return carry

    lax.fori_loop(0, total_ref.shape[0], step, 0)


def gather(ref, blocks, base=0):
    return jnp.concatenate(
        [ref[b >> 1, pl.ds(pl.multiple_of((b & 1) * BLK + base, BLK), BLK), :] for b in blocks], 0
    )


def probs_kernel(
    listed, pattern, live, order, query_ref, key_ref, grad_ref, probs_ref, key_t_ref, out_ref, total_ref
):
    scale = DH ** (-0.5) * math.log2(math.e)
    step, steps = pl.program_id(0), pl.num_programs(0)

    @pl.when(step == 0)
    def _():
        clear(total_ref)

    def group_step(group, carry):
        slots = [group * TOGETHER + t for t in range(TOGETHER)]
        tiles = [order[step * GROUP + slot] for slot in slots]

        def body(size):
            held = []
            for slot, tile in zip(slots, tiles):
                query = query_ref[rows_of(tile)]
                blocks = [pattern[tile * listed + j] for j in range(size)]
                scores = lax.dot_general(
                    gather(key_ref, blocks), query, NT, preferred_element_type=F32
                )
                key_block = lax.broadcasted_iota(jnp.int32, scores.shape, 0) >> 7
                scores = jnp.where(key_block < live[tile], scores, -jnp.inf)
                top = jnp.max(scores, axis=0, keepdims=True)
                weights = jnp.exp2((scores - top) * scale)
                inverse = 1.0 / jnp.sum(weights, axis=0, keepdims=True)
                probs = (weights * inverse).astype(BF16)
                probs_ref[slot, : size * BLK, :] = probs
                terms = jnp.dot(probs, grad_ref[rows_of(tile)], preferred_element_type=F32)
                held.append((blocks, terms))
            for blocks, terms in held:
                for j, b in enumerate(blocks):
                    total_ref[b] += terms[j * BLK : (j + 1) * BLK, :]

        by_count(live[tiles[0]], listed, body)
        for slot in slots:
            key_t_ref[slot] = key_ref[rows_of(step * GROUP + slot)].T
        return carry

    lax.fori_loop(0, GROUP // TOGETHER, group_step, 0)

    @pl.when(step == steps - 1)
    def _():
        def finish(block, carry):
            out_ref[rows_of(block)] = total_ref[block].astype(BF16)
            return carry

        lax.fori_loop(0, total_ref.shape[0], finish, 0)


def whole(shape, index=None):
    index = (0,) * len(shape) if index is None else index
    return pl.BlockSpec(shape, lambda i, *_: index, pipeline_mode=pl.Buffered(1))


def probs_of(query, pair, pattern, live_blocks, order, spare):
    tiles, listed = pattern.shape
    pairs = tiles * listed
    devices, rows, _ = query.shape
    return pl.pallas_call(
        functools.partial(probs_kernel, listed),
        grid_spec=pltpu.PrefetchScalarGridSpec(
            num_scalar_prefetch=3,
            grid=(tiles // GROUP,),
            in_specs=[whole(query.shape), whole(query.shape), whole(query.shape, (0, 1, 0))],
            out_specs=[
                pl.BlockSpec((GROUP, listed * BLK, BLK), lambda i, *_: (i, 0, 0)),
                pl.BlockSpec((GROUP, DH, BLK), lambda i, *_: (i, 0, 0)),
                whole((devices, rows + spare, DH)),
            ],
            scratch_shapes=[pltpu.VMEM((tiles, BLK, DH), F32)],
        ),
        out_shape=[
            jax.ShapeDtypeStruct((tiles, listed * BLK, BLK), BF16),
            jax.ShapeDtypeStruct((tiles, DH, BLK), BF16),
            jax.ShapeDtypeStruct((devices, rows + spare, DH), BF16),
        ],
        compiler_params=pltpu.CompilerParams(vmem_limit_bytes=KERNEL_LIMIT),
        cost_estimate=pl.CostEstimate(
            flops=4 * pairs * BLK * BLK * DH,
            bytes_accessed=2 * pairs * BLK * BLK,
            transcendentals=pairs * BLK * BLK,
        ),
    )(pattern.reshape(-1), live_blocks, order, query, pair, pair)


def grads_kernel(
    listed, pattern, live, order, query_ref, grad_ref, value_ref, key_t_ref, probs_ref, out_ref, total_ref
):
    scale = DH ** (-0.5)
    step, steps = pl.program_id(0), pl.num_programs(0)
    rows = query_ref.shape[1]

    @pl.when(step == 0)
    def _():
        clear(total_ref)

    def group_step(group, carry):
        slots = [group * TOGETHER + t for t in range(TOGETHER)]
        members = [order[step * GROUP + slot] for slot in slots]

        def body(size):
            held = []
            for slot, tile in zip(slots, members):
                blocks = [pattern[tile * listed + j] for j in range(size)]
                dprobs = lax.dot_general(
                    gather(value_ref, blocks), grad_ref[rows_of(tile)], NT, preferred_element_type=F32
                )
                probs = probs_ref[slot, : size * BLK, :].astype(F32)
                delta = jnp.sum(probs * dprobs, axis=0, keepdims=True)
                dscores = (probs * (dprobs - delta)).astype(BF16)
                keys_t = jnp.concatenate([key_t_ref[b] for b in blocks], 1)
                query_grad = jnp.dot(keys_t, dscores, preferred_element_type=F32)
                out_ref[rows_of(tile)] = (query_grad * scale).T.astype(BF16)
                terms = jnp.dot(dscores, query_ref[rows_of(tile)], preferred_element_type=F32)
                held.append((blocks, terms))
            for blocks, terms in held:
                for j, b in enumerate(blocks):
                    total_ref[b] += terms[j * BLK : (j + 1) * BLK, :]

        by_count(live[members[0]], listed, body)
        return carry

    lax.fori_loop(0, GROUP // TOGETHER, group_step, 0)

    @pl.when(step == steps - 1)
    def _():
        def finish(block, carry):
            start = pl.multiple_of((block & 1) * BLK + rows, BLK)
            out_ref[block >> 1, pl.ds(start, BLK), :] = (total_ref[block] * scale).astype(BF16)
            return carry

        lax.fori_loop(0, total_ref.shape[0], finish, 0)


def grads_of(query, pair, values, keys_t, probs, pattern, live_blocks, order):
    tiles, listed = pattern.shape
    pairs = tiles * listed
    devices, rows, _ = query.shape
    return pl.pallas_call(
        functools.partial(grads_kernel, listed),
        grid_spec=pltpu.PrefetchScalarGridSpec(
            num_scalar_prefetch=3,
            grid=(tiles // GROUP,),
            in_specs=[
                whole(query.shape),
                whole(query.shape, (0, 1, 0)),
                whole(query.shape),
                whole(keys_t.shape),
                pl.BlockSpec((GROUP, listed * BLK, BLK), lambda i, *_: (i, 0, 0)),
            ],
            out_specs=whole((devices, 2 * rows, DH)),
            scratch_shapes=[pltpu.VMEM((tiles, BLK, DH), F32)],
        ),
        out_shape=jax.ShapeDtypeStruct((devices, 2 * rows, DH), BF16),
        compiler_params=pltpu.CompilerParams(vmem_limit_bytes=KERNEL_LIMIT),
        cost_estimate=pl.CostEstimate(
            flops=6 * pairs * BLK * BLK * DH,
            bytes_accessed=2 * pairs * BLK * BLK + 16 * tiles * BLK * DH,
            transcendentals=0,
        ),
    )(pattern.reshape(-1), live_blocks, order, query, pair, values, keys_t, probs)


def exchange(blocks):
    return lax.all_to_all(blocks, "ctx", split_axis=0, concat_axis=0, tiled=True)


def body(
    queries, keys, values, features, feat_grad, conv_weight, head_weight, pattern, live_blocks
):
    devices = lax.axis_size("ctx")
    frames, positions, channels = features.shape
    taps = conv_weight.shape[0]
    rows = frames * positions

    incoming = lax.ppermute(feat_grad, "ctx", [(i + 1, i) for i in range(devices - 1)])
    packed = pack(queries)
    packed, incoming, feat_grad = lax.optimization_barrier((packed, incoming, feat_grad))
    query = exchange(packed)

    order = order_by_count(live_blocks)
    extended = jnp.concatenate([feat_grad, incoming], 0)
    windows = [extended[k : k + frames].reshape(rows, channels) for k in range(taps)]
    summed = sum(
        lax.dot_general(windows[k], conv_weight[k], NT, preferred_element_type=F32)
        for k in range(taps)
    )
    flat_features = features.reshape(rows, channels)
    tap_terms = jnp.stack(
        [
            lax.dot_general(flat_features, windows[k], TN, preferred_element_type=F32)
            for k in range(taps)
        ],
        0,
    ).astype(BF16)
    share = tap_terms.size // devices // DH
    held = -(-share // 16) * 16
    tap_terms = jnp.pad(tap_terms.reshape(devices, share, DH), ((0, 0), (0, held - share), (0, 0)))
    pair = pack_project(keys, summed.astype(BF16), head_weight)
    value_taps = pack(values, tap_terms)
    pair, value_taps, query, order = lax.optimization_barrier((pair, value_taps, query, order))

    pair = exchange(pair)
    value_taps, pair = lax.optimization_barrier((value_taps, pair))
    value_taps = exchange(value_taps)
    probs, keys_t, value_grad = probs_of(query, pair, pattern, live_blocks, order, held)

    value_grad = exchange(share_sum(value_taps, value_grad, held))
    grads = grads_of(query, pair, value_taps, keys_t, probs, pattern, live_blocks, order)
    grads, value_grad = lax.optimization_barrier((grads, value_grad))
    grads = exchange(grads)

    grads, value_grad = lax.optimization_barrier((grads, value_grad))
    grad_queries, grad_keys, grad_values = unpack(grads, value_grad)
    tap_total = value_grad[:, rows : rows + share, :].reshape(conv_weight.shape).astype(F32)
    token_count = rows * devices
    conv_weight_grad = tap_total * (1.0 / math.sqrt(token_count))
    return (grad_queries, grad_keys, grad_values, conv_weight_grad)


def solution(mesh):
    placed = (
        P(("clip", "ctx"), None),
        P(("clip", "ctx"), None),
        P(("clip", "ctx"), None),
        P(("clip", "ctx"), None, None),
        P(("clip", "ctx"), None, None),
        P(),
        P(),
        P("clip", None),
        P("clip"),
    )
    return jax.shard_map(
        body,
        mesh=mesh,
        in_specs=placed,
        out_specs=(
            P(("clip", "ctx"), None),
            P(("clip", "ctx"), None),
            P(("clip", "ctx"), None),
            P("clip", None, None),
        ),
        check_vma=False,
    )
```

profile of v0, /device:TPU:0, one launch (start us, length us, event | category | flops | bytes accessed | tf_op | source)
XLA Modules:
  0.0 271.2 jit_solution(17708743710768740896)
XLA Ops:
  0.6 1.1 copy.26
  1.8 1.3 collective-permute-start
  3.1 1.6 copy-done.7
  4.7 2.3 shard_map.120
  7.0 3.2 %collective-permute-done = bf16[2,128,384]{1,2,0:T(8,128)(2,1)S(1)} collective-permute-done((bf16[2,128,384]{1,2,0:T(8,128)(2,1)S(1)}, bf16[2,128,384]{1,2,0:T(8,128)(2,1)S(1)}, u32[]{:S(2)}, u32[]{:S(2)}) %collective-permute-start) | collective-permute-done | bytes 196640 | tf_op jit(solution)/shard_map/ppermute | solution.py:419
  10.2 12.6 %all-to-all-start = ((bf16[32,256,128]{2,1,0:T(8,128)(2,1)}), bf16[32,256,128]{2,1,0:T(8,128)(2,1)}, u32[]{:S(2)}, u32[]{:S(2)}) async-start(bf16[32,256,128]{2,1,0:T(8,128)(2,1)} %shard_map.120), calls=%async_computation | async-start | bytes 4194304 | tf_op jit(solution)/shard_map/all_to_all | solution.py:408
  23.0 0.7 select_reduce_fusion.order
  23.9 0.8 copy.29
  24.7 0.8 copy.28
  26.5 2.2 copy.31
  28.7 1.7 convert_element_type.19
  30.5 2.7 shard_map.122
  33.2 1.6 copy-done.3
  35.4 0.3 copy-done.11
  35.8 1.0 fusion.6.grad_ref
  36.7 5.9 %shard_map.121 = bf16[32,512,128]{2,1,0:T(8,128)(2,1)} custom-call(bf16[256,4096]{1,0:T(8,128)(2,1)} %key_ref.1, bf16[256,384]{1,0:T(8,128)(2,1)} %fusion.6.grad_ref, bf16[4096,384]{1,0:T(8,128)(2,1)} %weight_ref.1), custom_call_target="tpu_custom_call" | custom-call | flops 805306368 | bytes 8388608 | tf_op jit(solution)/shard_map/pallas_call | solution.py:168
  42.6 11.8 %all-to-all-done.query_ref = bf16[32,256,128]{2,1,0:T(8,128)(2,1)} async-done(((bf16[32,256,128]{2,1,0:T(8,128)(2,1)}), bf16[32,256,128]{2,1,0:T(8,128)(2,1)}, u32[]{:S(2)}, u32[]{:S(2)}) %all-to-all-start) | async-done | bytes 2097184 | tf_op jit(solution)/shard_map/all_to_all | solution.py:408
  54.4 55.3 %all_to_all.25.key_ref.grad_ref = bf16[32,512,128]{2,1,0:T(8,128)(2,1)} all-to-all(bf16[32,512,128]{2,1,0:T(8,128)(2,1)} %shard_map.121), channel_id=1, replica_groups=mesh['clip'=4,'ctx'=32] {'ctx'}, dimensions={0} | all-to-all | bytes 8388608 | tf_op jit(solution)/shard_map/all_to_all | solution.py:408
  109.6 4.4 %all-to-all-start.2 = ((bf16[32,368,128]{2,1,0:T(8,128)(2,1)}), bf16[32,368,128]{2,1,0:T(8,128)(2,1)S(1)}, u32[]{:S(2)}, u32[]{:S(2)}) async-start(bf16[32,368,128]{2,1,0:T(8,128)(2,1)} %copy-done.3), calls=%async_computation.2 | async-start | bytes 6029312 | tf_op jit(solution)/shard_map/all_to_all | solution.py:408
  114.1 0.7 reshape.32.pattern
  114.8 27.9 %shard_map.123 = (bf16[64,1024,128]{2,1,0:T(8,128)(2,1)}, bf16[64,128,128]{2,1,0:T(8,128)(2,1)}, bf16[32,368,128]{2,1,0:T(8,128)(2,1)}) custom-call(s32[512]{0:T(512)} %reshape.32.pattern, s32[64]{0:T(128)} %live.3, s32[64]{0:T(128)} %select_reduce_fusion.order, bf16[32,256,128]{2,1,0:T(8,128)(2,1)} %all-to-all-done.query_ref, ...), custom_call_target="tpu_custom_call" | custom-call | flops 4294967296 | bytes 16777216 | tf_op jit(solution)/shard_map/pallas_call | solution.py:302
  142.6 13.7 %all-to-all-done.2.value_ref.terms_ref = bf16[32,368,128]{2,1,0:T(8,128)(2,1)S(1)} async-done(((bf16[32,368,128]{2,1,0:T(8,128)(2,1)}), bf16[32,368,128]{2,1,0:T(8,128)(2,1)S(1)}, u32[]{:S(2)}, u32[]{:S(2)}) %all-to-all-start.2) | async-done | bytes 3014688 | tf_op jit(solution)/shard_map/all_to_all | solution.py:408
  156.4 2.9 %copy-done.4 = bf16[32,368,128]{2,1,0:T(8,128)(2,1)S(1)} copy-done((bf16[32,368,128]{2,1,0:T(8,128)(2,1)S(1)}, bf16[32,368,128]{2,1,0:T(8,128)(2,1)}, u32[]{:S(2)}) %copy-start.4) | copy-done | bytes 3014680
  159.3 1.7 shard_map.125
  161.1 1.7 copy-done.5
  162.7 4.3 %all-to-all-start.3 = ((bf16[32,368,128]{2,1,0:T(8,128)(2,1)}), bf16[32,368,128]{2,1,0:T(8,128)(2,1)S(1)}, u32[]{:S(2)}, u32[]{:S(2)}) async-start(bf16[32,368,128]{2,1,0:T(8,128)(2,1)} %copy-done.5), calls=%async_computation.3 | async-start | bytes 6029312 | tf_op jit(solution)/shard_map/all_to_all | solution.py:408
  167.0 31.9 %shard_map.124 = bf16[32,512,128]{2,1,0:T(8,128)(2,1)} custom-call(s32[512]{0:T(512)} %reshape.32.pattern, s32[64]{0:T(128)} %live.3, s32[64]{0:T(128)} %select_reduce_fusion.order, bf16[32,256,128]{2,1,0:T(8,128)(2,1)} %all-to-all-done.query_ref, bf16[32,512,128]{2,1,0:T(8,128)(2,1)} %all_to_all.25.key_ref.grad_ref, bf16[32,368,128]{2,1,0:T(8,128)(2,1)} %copy-done.2, ...), custom_call_target="tpu_custom_call" | custom-call | flops 6442450944 | bytes 33554432 | tf_op jit(solution)/shard_map/pallas_call | solution.py:382
  198.9 8.6 %all-to-all-done.3.last_ref = bf16[32,368,128]{2,1,0:T(8,128)(2,1)S(1)} async-done(((bf16[32,368,128]{2,1,0:T(8,128)(2,1)}), bf16[32,368,128]{2,1,0:T(8,128)(2,1)S(1)}, u32[]{:S(2)}, u32[]{:S(2)}) %all-to-all-start.3) | async-done | bytes 3014688 | tf_op jit(solution)/shard_map/all_to_all | solution.py:408
  207.5 55.5 %all_to_all.26.pair_ref = bf16[32,512,128]{2,1,0:T(8,128)(2,1)S(1)} all-to-all(bf16[32,512,128]{2,1,0:T(8,128)(2,1)} %shard_map.124), channel_id=1, replica_groups=mesh['clip'=4,'ctx'=32] {'ctx'}, dimensions={0} | all-to-all | bytes 8388608 | tf_op jit(solution)/shard_map/all_to_all | solution.py:408
  263.0 1.4 convert_multiply_fusion
  264.4 4.0 %shard_map.126 = (bf16[256,4096]{1,0:T(8,128)(2,1)}, bf16[256,4096]{1,0:T(8,128)(2,1)}, bf16[256,4096]{1,0:T(8,128)(2,1)}) custom-call(bf16[32,512,128]{2,1,0:T(8,128)(2,1)S(1)} %all_to_all.26.pair_ref, bf16[32,368,128]{2,1,0:T(8,128)(2,1)S(1)} %all-to-all-done.3.last_ref), custom_call_target="tpu_custom_call" | custom-call | bytes 12582912 | tf_op jit(solution)/shard_map/pallas_call | solution.py:211
  268.4 2.7 %mul.18 = f32[3,384,384]{2,1,0:T(8,128)} reshape(f32[32,108,128]{2,1,0:T(8,128)} %convert_multiply_fusion) | data formatting | bytes 3538944 | tf_op jit(solution)/shard_map/mul | solution.py:460
  (34 shorter events, 2.1 us)
Async XLA Ops:
  0.6 24.9 %copy-start = (bf16[2,128,384]{2,1,0:T(8,128)(2,1)S(1)}, bf16[2,128,384]{2,1,0:T(8,128)(2,1)}, u32[]{:S(2)}) copy-start(bf16[2,128,384]{2,1,0:T(8,128)(2,1)} %param.12) | copy-start | bytes 589828
  1.8 8.4 %collective-permute-start = (bf16[2,128,384]{1,2,0:T(8,128)(2,1)S(1)}, bf16[2,128,384]{1,2,0:T(8,128)(2,1)S(1)}, u32[]{:S(2)}, u32[]{:S(2)}) collective-permute-start(bf16[2,128,384]{1,2,0:T(8,128)(2,1)S(1)} %copy.26), channel_id=1, source_target_pairs={{1,0},{2,1},{3,2},{4,3},{5,4},{6,5},{7,6},{8,7},{9,8},{10,9},{11,1... | collective-permute-start | bytes 589832 | tf_op jit(solution)/shard_map/ppermute | solution.py:419
  3.1 1.6 copy-start.7
  7.0 15.8 %copy-start.13 = (s32[64]{0:T(128)S(1)}, s32[64]{0:T(128)}, u32[]{:S(2)}) copy-start(s32[64]{0:T(128)} %live.3) | copy-start | bytes 772
  7.0 16.7 %copy-start.8 = (bf16[2,128,384]{2,1,0:T(8,128)(2,1)S(1)}, bf16[2,128,384]{2,1,0:T(8,128)(2,1)}, u32[]{:S(2)}) copy-start(bf16[2,128,384]{2,1,0:T(8,128)(2,1)} %param.13) | copy-start | bytes 589828
  10.2 44.2 %all-to-all-start = ((bf16[32,256,128]{2,1,0:T(8,128)(2,1)}), bf16[32,256,128]{2,1,0:T(8,128)(2,1)}, u32[]{:S(2)}, u32[]{:S(2)}) async-start(bf16[32,256,128]{2,1,0:T(8,128)(2,1)} %shard_map.120), calls=%async_computation | async-start | bytes 4194304 | tf_op jit(solution)/shard_map/all_to_all | solution.py:408
  28.7 1.9 copy-start.6
  30.5 4.3 %copy-start.9 = (bf16[3,384,384]{2,1,0:T(8,128)(2,1)S(1)}, bf16[3,384,384]{2,1,0:T(8,128)(2,1)}, u32[]{:S(2)}) copy-start(bf16[3,384,384]{2,1,0:T(8,128)(2,1)} %param.14) | copy-start | bytes 2654212
  30.5 4.3 %copy-start.10 = (bf16[2,128,384]{2,1,0:T(8,128)(2,1)S(1)}, bf16[2,128,384]{2,1,0:T(8,128)(2,1)}, u32[]{:S(2)}) copy-start(bf16[2,128,384]{2,1,0:T(8,128)(2,1)} %copy.28) | copy-start | bytes 589828
  33.2 1.6 copy-start.3
  34.8 0.9 copy-start.11
  109.6 4.4 %copy-start.12 = (s32[64,8]{0,1:T(8,128)S(1)}, s32[64,8]{0,1:T(8,128)}, u32[]{:S(2)}) copy-start(s32[64,8]{0,1:T(8,128)} %param.16) | copy-start | bytes 6148
  109.6 46.7 %all-to-all-start.2 = ((bf16[32,368,128]{2,1,0:T(8,128)(2,1)}), bf16[32,368,128]{2,1,0:T(8,128)(2,1)S(1)}, u32[]{:S(2)}, u32[]{:S(2)}) async-start(bf16[32,368,128]{2,1,0:T(8,128)(2,1)} %copy-done.3), calls=%async_computation.2 | async-start | bytes 6029312 | tf_op jit(solution)/shard_map/all_to_all | solution.py:408
  156.4 4.7 %copy-start.2 = (bf16[32,368,128]{2,1,0:T(8,128)(2,1)}, bf16[32,368,128]{2,1,0:T(8,128)(2,1)S(1)}, u32[]{:S(2)}) copy-start(bf16[32,368,128]{2,1,0:T(8,128)(2,1)S(1)} %all-to-all-done.2.value_ref.terms_ref) | copy-start | bytes 9043972
  156.4 2.9 %copy-start.4 = (bf16[32,368,128]{2,1,0:T(8,128)(2,1)S(1)}, bf16[32,368,128]{2,1,0:T(8,128)(2,1)}, u32[]{:S(2)}) copy-start(bf16[32,368,128]{2,1,0:T(8,128)(2,1)} %get-tuple-element.34.into_ref) | copy-start | bytes 9043972
  161.0 1.7 copy-start.5
  162.7 44.7 %all-to-all-start.3 = ((bf16[32,368,128]{2,1,0:T(8,128)(2,1)}), bf16[32,368,128]{2,1,0:T(8,128)(2,1)S(1)}, u32[]{:S(2)}, u32[]{:S(2)}) async-start(bf16[32,368,128]{2,1,0:T(8,128)(2,1)} %copy-done.5), calls=%async_computation.3 | async-start | bytes 6029312 | tf_op jit(solution)/shard_map/all_to_all | solution.py:408
  264.4 6.8 %copy-start.1 = (bf16[2,128,384]{2,1,0:T(8,128)(2,1)S(1)}, bf16[2,128,384]{2,1,0:T(8,128)(2,1)}, u32[]{:S(2)}) copy-start(bf16[2,128,384]{2,1,0:T(8,128)(2,1)} %param.12) | copy-start | bytes 589828
where the time goes:
time: 272 us; the launch traced here: 271 us
  blocking collectives  111 us (41%)
  Pallas kernels  76.3 us (28%)
  waiting for transfers between devices  37.2 us (14%)
  starting transfers between devices  22.6 us (8%)
  local copies, waits for them, and re-layouts  18.6 us (7%)
    all_to_all x2, blocking collectives, exchange(): lax.all_to_all(blocks, 'ctx', split_axis=0, concat_axis=0, tiled=True)  111 us
    all_to_all x3, waiting for transfers between devices, exchange(): lax.all_to_all(blocks, 'ctx', split_axis=0, concat_axis=0, tiled=True)  34.1 us
    pallas_call x1, Pallas kernels, grads_of(): pl.pallas_call(functools.partial(grads_kernel, listed), grid_spec=pltpu.P...  31.9 us
    pallas_call x1, Pallas kernels, probs_of(): pl.pallas_call(functools.partial(probs_kernel, listed), grid_spec=pltpu.P...  27.9 us
    all_to_all x3, starting transfers between devices, exchange(): lax.all_to_all(blocks, 'ctx', split_axis=0, concat_axis=0, tiled=True)  21.3 us
    unnamed x30, local copies, waits for them, and re-layouts  9.44 us
    pallas_call x1, Pallas kernels, pack_project(): pl.pallas_call(pack_project_kernel, in_specs=[HBM_SPEC, VMEM_SPEC, VMEM_S...  5.88 us
  transfers between devices with their start and end apart: 4, of which 4 were waited for; matrix products, arithmetic and copies ran while one was open for 4% of the time, Pallas kernels for 26%

commit v1 on v0

--- a/solution.py
+++ b/solution.py
@@ -19,6 +19,7 @@
 BF16 = jnp.bfloat16
 KERNEL_LIMIT = 56 * 1024 * 1024
 SMALL_LIMIT = 16 * 1024 * 1024
+MEDIUM_LIMIT = 32 * 1024 * 1024
 HBM_SPEC = pl.BlockSpec(memory_space=pl.ANY)
 VMEM_SPEC = pl.BlockSpec(memory_space=pltpu.VMEM)
 
@@ -40,6 +41,10 @@
     rank = jnp.sum(ahead.astype(jnp.int32), axis=1)
     placed = (rank[None, :] == ids[:, None]).astype(jnp.int32)
     return jnp.sum(placed * ids[None, :], axis=1)
+
+
+def in_hbm(array):
+    return pltpu.with_memory_space_constraint(array, pltpu.HBM)
 
 
 def columns_of(ref, head):
@@ -60,50 +65,145 @@
             copy.wait()
 
 
-def pack_kernel(array_ref, *refs):
-    *tap_refs, out_ref, held_ref, in_sems, out_sems = refs
-    rows = array_ref.shape[0]
+def pack_kernel(query_ref, key_ref, value_ref, triple_ref, last_ref, held_ref, in_sems, out_sems):
+    rows = query_ref.shape[0]
     stages = []
-    for first in range(0, out_ref.shape[0], PACKED):
+    for first in range(0, held_ref.shape[0], PACKED):
         heads = pl.ds(first, PACKED)
         arrivals = [
             pltpu.make_async_copy(
-                columns_of(array_ref, head), held_ref.at[head, pl.ds(0, rows), :], in_sems.at[head]
+                columns_of(ref, head),
+                held_ref.at[head, pl.ds(place * rows, rows), :],
+                in_sems.at[place, head],
             )
             for head in range(first, first + PACKED)
+            for place, ref in enumerate((query_ref, key_ref, value_ref))
         ]
-        for tap_ref in tap_refs:
-            arrivals.append(
-                pltpu.make_async_copy(
-                    tap_ref.at[heads],
-                    held_ref.at[heads, pl.ds(rows, tap_ref.shape[1]), :],
-                    in_sems.at[out_ref.shape[0] + first // PACKED],
-                )
-            )
-        leaving = pltpu.make_async_copy(
-            held_ref.at[heads], out_ref.at[heads], out_sems.at[first // PACKED]
-        )
-        stages.append((arrivals, [leaving]))
+        departures = [
+            pltpu.make_async_copy(
+                held_ref.at[heads, pl.ds(0, 2 * rows), :],
+                triple_ref.at[heads, pl.ds(0, 2 * rows), :],
+                out_sems.at[0, first // PACKED],
+            ),
+            pltpu.make_async_copy(
+                held_ref.at[heads, pl.ds(2 * rows, rows), :],
+                last_ref.at[heads, pl.ds(0, rows), :],
+                out_sems.at[1, first // PACKED],
+            ),
+        ]
+        stages.append((arrivals, departures))
     relay(stages)
 
 
-def pack(array, *taps):
-    rows, width = array.shape
+def pack(queries, keys, values, held):
+    rows, width = queries.shape
     heads = width // DH
-    shape = (heads, rows + sum(tap.shape[1] for tap in taps), DH)
     return pl.pallas_call(
         pack_kernel,
-        in_specs=[HBM_SPEC] * (1 + len(taps)),
-        out_specs=HBM_SPEC,
-        out_shape=jax.ShapeDtypeStruct(shape, array.dtype),
+        in_specs=[HBM_SPEC] * 3,
+        out_specs=[HBM_SPEC] * 2,
+        out_shape=[
+            pltpu.HBM((heads, 3 * rows, DH), BF16),
+            pltpu.HBM((heads, rows + held, DH), BF16),
+        ],
         scratch_shapes=[
-            pltpu.VMEM(shape, array.dtype),
-            pltpu.SemaphoreType.DMA((heads + heads // PACKED,)),
-            pltpu.SemaphoreType.DMA((heads // PACKED,)),
+            pltpu.VMEM((heads, 3 * rows, DH), BF16),
+            pltpu.SemaphoreType.DMA((3, heads)),
+            pltpu.SemaphoreType.DMA((2, heads // PACKED)),
         ],
         compiler_params=pltpu.CompilerParams(vmem_limit_bytes=SMALL_LIMIT),
-        cost_estimate=pl.CostEstimate(flops=0, bytes_accessed=4 * rows * width, transcendentals=0),
-    )(array, *taps)
+        cost_estimate=pl.CostEstimate(flops=0, bytes_accessed=12 * rows * width, transcendentals=0),
+    )(in_hbm(queries), in_hbm(keys), in_hbm(values))
+
+
+def decoder_kernel(
+    near_ref,
+    next_ref,
+    feature_ref,
+    tap_weight_ref,
+    head_weight_ref,
+    triple_in_ref,
+    last_in_ref,
+    triple_ref,
+    last_ref,
+    held_ref,
+    taps_ref,
+    grad_sems,
+    tap_sems,
+):
+    heads, rows, _ = held_ref.shape
+    frames, positions, channels = feature_ref.shape
+    devices = last_ref.shape[0]
+    share = taps_ref.shape[0] // devices
+    steps = [near_ref[f] for f in range(frames)] + [next_ref[f] for f in range(frames)]
+    taps = tap_weight_ref.shape[0]
+    windows = [jnp.concatenate(steps[k : k + frames], 0) for k in range(taps)]
+    feature_grad = sum(
+        lax.dot_general(windows[k], tap_weight_ref[k], NT, preferred_element_type=F32)
+        for k in range(taps)
+    ).astype(BF16)
+    copies = []
+    for first in range(0, heads, PACKED):
+        projected = lax.dot_general(
+            feature_grad,
+            head_weight_ref[first * DH : (first + PACKED) * DH, :],
+            NT,
+            preferred_element_type=F32,
+        ).astype(BF16)
+        for head in range(PACKED):
+            held_ref[first + head] = projected[:, head * DH : (head + 1) * DH]
+        group = pl.ds(first, PACKED)
+        copies.append(
+            pltpu.make_async_copy(
+                held_ref.at[group],
+                triple_ref.at[group, pl.ds(2 * rows, rows), :],
+                grad_sems.at[first // PACKED],
+            )
+        )
+        copies[-1].start()
+    features_t = jnp.concatenate([feature_ref[f] for f in range(frames)], 0).T
+    row = 0
+    for k in range(taps):
+        terms = jnp.dot(features_t, windows[k], preferred_element_type=F32).astype(BF16)
+        for first in range(0, channels, DH):
+            taps_ref[row : row + channels, :] = terms[:, first : first + DH]
+            row += channels
+    taps_ref[row:, :] = jnp.zeros((taps_ref.shape[0] - row, DH), BF16)
+    for device in range(devices):
+        copies.append(
+            pltpu.make_async_copy(
+                taps_ref.at[pl.ds(device * share, share), :],
+                last_ref.at[device, pl.ds(rows, share), :],
+                tap_sems.at[device],
+            )
+        )
+        copies[-1].start()
+    for copy in copies:
+        copy.wait()
+
+
+def decoder(feat_grad, incoming, features, conv_weight, head_weight, triple, last):
+    heads, rows = triple.shape[0], triple.shape[1] // 3
+    share = last.shape[1] - rows
+    return pl.pallas_call(
+        decoder_kernel,
+        in_specs=[VMEM_SPEC] * 5 + [HBM_SPEC] * 2,
+        out_specs=[HBM_SPEC] * 2,
+        out_shape=[pltpu.HBM(x.shape, x.dtype) for x in (triple, last)],
+        scratch_shapes=[
+            pltpu.VMEM((heads, rows, DH), BF16),
+            pltpu.VMEM((heads * share, DH), BF16),
+            pltpu.SemaphoreType.DMA((heads // PACKED,)),
+            pltpu.SemaphoreType.DMA((heads,)),
+        ],
+        input_output_aliases={5: 0, 6: 1},
+        compiler_params=pltpu.CompilerParams(vmem_limit_bytes=MEDIUM_LIMIT),
+        cost_estimate=pl.CostEstimate(
+            flops=2 * heads * rows * DH * head_weight.shape[1],
+            bytes_accessed=6 * heads * rows * DH,
+            transcendentals=0,
+        ),
+    )(feat_grad, incoming, features, conv_weight, head_weight, in_hbm(triple), in_hbm(last))
 
 
 def share_sum_kernel(terms_ref, into_ref, out_ref, terms, total, in_sem, out_sems):
@@ -129,7 +229,7 @@
         share_sum_kernel,
         in_specs=[HBM_SPEC] * 2,
         out_specs=HBM_SPEC,
-        out_shape=jax.ShapeDtypeStruct(into.shape, into.dtype),
+        out_shape=pltpu.HBM(into.shape, into.dtype),
         scratch_shapes=[
             pltpu.VMEM((devices, held, DH), BF16),
             pltpu.VMEM((held, DH), BF16),
@@ -138,49 +238,21 @@
         ],
         input_output_aliases={1: 0},
         compiler_params=pltpu.CompilerParams(vmem_limit_bytes=SMALL_LIMIT),
-    )(terms, into)
-
-
-def pack_project_kernel(key_ref, grad_ref, weight_ref, out_ref, sems):
-    heads, rows = out_ref.shape[0], key_ref.shape[0]
-    copies = [
+    )(in_hbm(terms), in_hbm(into))
+
+
+def unpack_kernel(factor, pair_ref, last_ref, *refs):
+    *out_refs, tap_out_ref, held_ref, taps_ref, scaled_ref, in_sems, out_sems, tap_sems, done_sem = refs
+    heads, rows = held_ref.shape[0], out_refs[0].shape[0]
+    share = last_ref.shape[1] - rows
+    tap_copies = [
         pltpu.make_async_copy(
-            columns_of(key_ref, head), out_ref.at[head, pl.ds(0, rows), :], sems.at[head]
+            last_ref.at[device, pl.ds(rows, share), :],
+            taps_ref.at[pl.ds(device * share, share), :],
+            tap_sems.at[device],
         )
-        for head in range(heads)
+        for device in range(heads)
     ]
-    for copy in copies:
-        copy.start()
-    for head in range(0, heads, 2):
-        projected = lax.dot_general(
-            grad_ref[...], weight_ref[head * DH : (head + 2) * DH, :], NT, preferred_element_type=F32
-        ).astype(BF16)
-        out_ref[head, rows:, :] = projected[:, :DH]
-        out_ref[head + 1, rows:, :] = projected[:, DH:]
-    for copy in copies:
-        copy.wait()
-
-
-def pack_project(keys, feature_grad, head_weight):
-    rows, width = keys.shape
-    heads = width // DH
-    channels = feature_grad.shape[1]
-    return pl.pallas_call(
-        pack_project_kernel,
-        in_specs=[HBM_SPEC, VMEM_SPEC, VMEM_SPEC],
-        out_specs=VMEM_SPEC,
-        out_shape=jax.ShapeDtypeStruct((heads, 2 * rows, DH), keys.dtype),
-        scratch_shapes=[pltpu.SemaphoreType.DMA((heads,))],
-        compiler_params=pltpu.CompilerParams(vmem_limit_bytes=KERNEL_LIMIT),
-        cost_estimate=pl.CostEstimate(
-            flops=2 * rows * width * channels, bytes_accessed=8 * rows * width, transcendentals=0
-        ),
-    )(keys, feature_grad, head_weight)
-
-
-def unpack_kernel(pair_ref, last_ref, *refs):
-    *out_refs, held_ref, in_sems, out_sems = refs
-    heads, rows = held_ref.shape[0], out_refs[0].shape[0]
     stages = []
     for first in range(0, heads, PACKED):
         group = pl.ds(first, PACKED)
@@ -203,26 +275,55 @@
             for place, out_ref in enumerate(out_refs)
         ]
         stages.append((arrivals, departures))
-    relay(stages)
-
-
-def unpack(pair, last):
+    for arrivals, _ in stages:
+        for copy in arrivals:
+            copy.start()
+    for copy in tap_copies:
+        copy.start()
+    for arrivals, departures in stages:
+        for copy in arrivals:
+            copy.wait()
+        for copy in departures:
+            copy.start()
+    for copy in tap_copies:
+        copy.wait()
+    taps, channels, width = scaled_ref.shape
+    row = 0
+    for k in range(taps):
+        for first in range(0, width, DH):
+            terms = taps_ref[row : row + channels, :].astype(F32) * factor
+            scaled_ref[k, :, first : first + DH] = terms
+            row += channels
+    done = pltpu.make_async_copy(scaled_ref, tap_out_ref, done_sem)
+    done.start()
+    for _, departures in stages:
+        for copy in departures:
+            copy.wait()
+    done.wait()
+
+
+def unpack(pair, last, tap_shape, factor):
     heads, rows = pair.shape[0], pair.shape[1] // 2
     return pl.pallas_call(
-        unpack_kernel,
+        functools.partial(unpack_kernel, factor),
         in_specs=[HBM_SPEC] * 2,
-        out_specs=[HBM_SPEC] * 3,
-        out_shape=[jax.ShapeDtypeStruct((rows, heads * DH), last.dtype)] * 3,
+        out_specs=[HBM_SPEC] * 4,
+        out_shape=[jax.ShapeDtypeStruct((rows, heads * DH), last.dtype)] * 3
+        + [jax.ShapeDtypeStruct(tap_shape, F32)],
         scratch_shapes=[
             pltpu.VMEM((heads, 3 * rows, DH), last.dtype),
+            pltpu.VMEM((heads * (last.shape[1] - rows), DH), last.dtype),
+            pltpu.VMEM(tap_shape, F32),
             pltpu.SemaphoreType.DMA((2, heads // PACKED)),
             pltpu.SemaphoreType.DMA((3, heads)),
+            pltpu.SemaphoreType.DMA((heads,)),
+            pltpu.SemaphoreType.DMA(()),
         ],
         compiler_params=pltpu.CompilerParams(vmem_limit_bytes=SMALL_LIMIT),
         cost_estimate=pl.CostEstimate(
             flops=0, bytes_accessed=12 * rows * heads * DH, transcendentals=0
         ),
-    )(pair, last)
+    )(in_hbm(pair), in_hbm(last))
 
 
 def clear(total_ref):
@@ -295,16 +396,17 @@
     return pl.BlockSpec(shape, lambda i, *_: index, pipeline_mode=pl.Buffered(1))
 
 
-def probs_of(query, pair, pattern, live_blocks, order, spare):
+def probs_of(triple, pattern, live_blocks, order, spare):
     tiles, listed = pattern.shape
     pairs = tiles * listed
-    devices, rows, _ = query.shape
+    devices, rows = triple.shape[0], triple.shape[1] // 3
+    part = (devices, rows, DH)
     return pl.pallas_call(
         functools.partial(probs_kernel, listed),
         grid_spec=pltpu.PrefetchScalarGridSpec(
             num_scalar_prefetch=3,
             grid=(tiles // GROUP,),
-            in_specs=[whole(query.shape), whole(query.shape), whole(query.shape, (0, 1, 0))],
+            in_specs=[whole(part, (0, place, 0)) for place in range(3)],
             out_specs=[
                 pl.BlockSpec((GROUP, listed * BLK, BLK), lambda i, *_: (i, 0, 0)),
                 pl.BlockSpec((GROUP, DH, BLK), lambda i, *_: (i, 0, 0)),
@@ -315,7 +417,7 @@
         out_shape=[
             jax.ShapeDtypeStruct((tiles, listed * BLK, BLK), BF16),
             jax.ShapeDtypeStruct((tiles, DH, BLK), BF16),
-            jax.ShapeDtypeStruct((devices, rows + spare, DH), BF16),
+            pltpu.HBM((devices, rows + spare, DH), BF16),
         ],
         compiler_params=pltpu.CompilerParams(vmem_limit_bytes=KERNEL_LIMIT),
         cost_estimate=pl.CostEstimate(
@@ -323,7 +425,7 @@
             bytes_accessed=2 * pairs * BLK * BLK,
             transcendentals=pairs * BLK * BLK,
         ),
-    )(pattern.reshape(-1), live_blocks, order, query, pair, pair)
+    )(pattern.reshape(-1), live_blocks, order, triple, triple, triple)
 
 
 def grads_kernel(
@@ -375,19 +477,20 @@
         lax.fori_loop(0, total_ref.shape[0], finish, 0)
 
 
-def grads_of(query, pair, values, keys_t, probs, pattern, live_blocks, order):
+def grads_of(triple, values, keys_t, probs, pattern, live_blocks, order):
     tiles, listed = pattern.shape
     pairs = tiles * listed
-    devices, rows, _ = query.shape
+    devices, rows = triple.shape[0], triple.shape[1] // 3
+    part = (devices, rows, DH)
     return pl.pallas_call(
         functools.partial(grads_kernel, listed),
         grid_spec=pltpu.PrefetchScalarGridSpec(
             num_scalar_prefetch=3,
             grid=(tiles // GROUP,),
             in_specs=[
-                whole(query.shape),
-                whole(query.shape, (0, 1, 0)),
-                whole(query.shape),
+                whole(part),
+                whole(part, (0, 2, 0)),
+                whole(part),
                 whole(keys_t.shape),
                 pl.BlockSpec((GROUP, listed * BLK, BLK), lambda i, *_: (i, 0, 0)),
             ],
@@ -401,7 +504,7 @@
             bytes_accessed=2 * pairs * BLK * BLK + 16 * tiles * BLK * DH,
             transcendentals=0,
         ),
-    )(pattern.reshape(-1), live_blocks, order, query, pair, values, keys_t, probs)
+    )(pattern.reshape(-1), live_blocks, order, triple, triple, values, keys_t, probs)
 
 
 def exchange(blocks):
@@ -413,52 +516,31 @@
 ):
     devices = lax.axis_size("ctx")
     frames, positions, channels = features.shape
-    taps = conv_weight.shape[0]
     rows = frames * positions
+    share = -(-conv_weight.size // devices // DH // 16) * 16
 
     incoming = lax.ppermute(feat_grad, "ctx", [(i + 1, i) for i in range(devices - 1)])
-    packed = pack(queries)
-    packed, incoming, feat_grad = lax.optimization_barrier((packed, incoming, feat_grad))
-    query = exchange(packed)
-
     order = order_by_count(live_blocks)
-    extended = jnp.concatenate([feat_grad, incoming], 0)
-    windows = [extended[k : k + frames].reshape(rows, channels) for k in range(taps)]
-    summed = sum(
-        lax.dot_general(windows[k], conv_weight[k], NT, preferred_element_type=F32)
-        for k in range(taps)
+    triple, value_taps = pack(queries, keys, values, share)
+    triple, value_taps, order, incoming = lax.optimization_barrier(
+        (triple, value_taps, order, incoming)
     )
-    flat_features = features.reshape(rows, channels)
-    tap_terms = jnp.stack(
-        [
-            lax.dot_general(flat_features, windows[k], TN, preferred_element_type=F32)
-            for k in range(taps)
-        ],
-        0,
-    ).astype(BF16)
-    share = tap_terms.size // devices // DH
-    held = -(-share // 16) * 16
-    tap_terms = jnp.pad(tap_terms.reshape(devices, share, DH), ((0, 0), (0, held - share), (0, 0)))
-    pair = pack_project(keys, summed.astype(BF16), head_weight)
-    value_taps = pack(values, tap_terms)
-    pair, value_taps, query, order = lax.optimization_barrier((pair, value_taps, query, order))
-
-    pair = exchange(pair)
-    value_taps, pair = lax.optimization_barrier((value_taps, pair))
+    triple, value_taps = decoder(
+        feat_grad, incoming, features, conv_weight, head_weight, triple, value_taps
+    )
+
+    triple = exchange(triple)
+    value_taps, triple = lax.optimization_barrier((value_taps, triple))
     value_taps = exchange(value_taps)
-    probs, keys_t, value_grad = probs_of(query, pair, pattern, live_blocks, order, held)
-
-    value_grad = exchange(share_sum(value_taps, value_grad, held))
-    grads = grads_of(query, pair, value_taps, keys_t, probs, pattern, live_blocks, order)
+    probs, keys_t, value_grad = probs_of(triple, pattern, live_blocks, order, share)
+
+    value_grad = exchange(share_sum(value_taps, value_grad, share))
+    grads = grads_of(triple, value_taps, keys_t, probs, pattern, live_blocks, order)
     grads, value_grad = lax.optimization_barrier((grads, value_grad))
     grads = exchange(grads)
 
-    grads, value_grad = lax.optimization_barrier((grads, value_grad))
-    grad_queries, grad_keys, grad_values = unpack(grads, value_grad)
-    tap_total = value_grad[:, rows : rows + share, :].reshape(conv_weight.shape).astype(F32)
-    token_count = rows * devices
-    conv_weight_grad = tap_total * (1.0 / math.sqrt(token_count))
-    return (grad_queries, grad_keys, grad_values, conv_weight_grad)
+    factor = 1.0 / math.sqrt(rows * devices)
+    return tuple(unpack(grads, value_grad, conv_weight.shape, factor))
 
 
 def solution(mesh):

time: 272 us -> 261 us (0.960)
  blocking collectives: 111 us -> 140 us
  local copies, waits for them, and re-layouts: 18.6 us -> 2.5 us
  waiting for transfers between devices: 37.2 us -> 21.1 us
  starting transfers between devices: 22.6 us -> 11.3 us
  Pallas kernels: 76.3 us -> 82 us
    all_to_all x2, blocking collectives: 111 us -> 140 us  [exchange(): lax.all_to_all(blocks, 'ctx', split_axis=0, concat_axis=0, tiled=True)]
    all_to_all x3 -> x2, waiting for transfers between devices: 34.1 us -> 21.1 us  [exchange(): lax.all_to_all(blocks, 'ctx', split_axis=0, concat_axis=0, tiled=True)]
    all_to_all x3 -> x2, starting transfers between devices: 21.3 us -> 9.75 us  [exchange(): lax.all_to_all(blocks, 'ctx', split_axis=0, concat_axis=0, tiled=True)]
    unnamed x30 -> x17, local copies, waits for them, and re-layouts: 9.44 us -> 1.83 us
    ppermute x1, waiting for transfers between devices: 3.16 us -> 0.05 us  [body(): lax.ppermute(feat_grad, 'ctx', [(i + 1, i) for i in range(devices - 1)])]
    mul x1 -> x0, local copies, waits for them, and re-layouts: 2.74 us -> none  [body(): conv_weight_grad = tap_total * (1.0 / math.sqrt(token_count))]
    pallas_call x4 -> x3, Pallas kernels: 14.8 us -> 17.3 us  [the longest x1 7.5 us: unpack(): pl.pallas_call(functools.partial(unpack_kernel, factor), in_specs=[HBM_SP...]
  transfers between devices with their start and end apart: 4 -> 3, of which waited for: 4 -> 3; matrix products, arithmetic and copies ran while one was open for 4% -> 1% of each run, Pallas kernels for 26% -> 26%
where the time goes in v1:
time: 261 us; the launch traced here: 258 us
  blocking collectives  140 us (54%)
  Pallas kernels  82 us (31%)
  waiting for transfers between devices  21.1 us (8%)
  starting transfers between devices  11.3 us (4%)
    all_to_all x2, blocking collectives, exchange(): lax.all_to_all(blocks, 'ctx', split_axis=0, concat_axis=0, tiled=True)  140 us
    pallas_call x1, Pallas kernels, grads_of(): pl.pallas_call(functools.partial(grads_kernel, listed), grid_spec=pltpu.P...  33.2 us
    pallas_call x1, Pallas kernels, probs_of(): pl.pallas_call(functools.partial(probs_kernel, listed), grid_spec=pltpu.P...  28.9 us
    all_to_all x2, waiting for transfers between devices, exchange(): lax.all_to_all(blocks, 'ctx', split_axis=0, concat_axis=0, tiled=True)  21.1 us
    all_to_all x2, starting transfers between devices, exchange(): lax.all_to_all(blocks, 'ctx', split_axis=0, concat_axis=0, tiled=True)  9.75 us
    pallas_call x1, Pallas kernels, unpack(): pl.pallas_call(functools.partial(unpack_kernel, factor), in_specs=[HBM_SP...  7.5 us
    pallas_call x1, Pallas kernels, pack(): pl.pallas_call(pack_kernel, in_specs=[HBM_SPEC] * 3, out_specs=[HBM_SPEC]...  6.4 us
  transfers between devices with their start and end apart: 3, of which 3 were waited for; matrix products, arithmetic and copies ran while one was open for 1% of the time, Pallas kernels for 26%

profile of v1, /device:TPU:0, one launch (start us, length us, event | category | flops | bytes accessed | tf_op | source)
XLA Modules:
  0.0 258.5 jit_solution(1588631574300117420)
XLA Ops:
  0.6 0.0 copy-start.2
  0.6 0.0 copy-start.7
  0.7 0.0 copy-start
  0.7 0.0 copy-start.1
  0.7 0.0 copy-start.3
  0.7 1.6 collective-permute-start
  2.2 6.4 %shard_map.120 = (bf16[32,768,128]{2,1,0:T(8,128)(2,1)}, bf16[32,368,128]{2,1,0:T(8,128)(2,1)}) custom-call(bf16[256,4096]{1,0:T(8,128)(2,1)} %query_ref.1, bf16[256,4096]{1,0:T(8,128)(2,1)} %key_ref.1, bf16[256,4096]{1,0:T(8,128)(2,1)} %value_ref.1), custom_call_target="tpu_custom_call" | custom-call | bytes 12582912 | tf_op jit(solution)/shard_map/pallas_call | solution.py:101
  8.7 0.0 copy-done.7
  8.7 0.2 convert_reduce_fusion
  8.8 0.6 select_reduce_fusion.order
  9.5 0.1 collective-permute-done.next_ref
  9.5 0.0 copy-done.2
  9.5 0.0 copy-done
  9.5 0.0 copy-done.1
  9.5 0.0 copy-done.3
  9.6 3.4 %shard_map.121 = (bf16[32,768,128]{2,1,0:T(8,128)(2,1)}, bf16[32,368,128]{2,1,0:T(8,128)(2,1)}) custom-call(bf16[2,128,384]{2,1,0:T(8,128)(2,1)S(1)} %copy-done.2, bf16[2,128,384]{2,1,0:T(8,128)(2,1)S(1)} %collective-permute-done.next_ref, bf16[2,128,384]{2,1,0:T(8,128)(2,1)S(1)} %copy-done.3, ...), custom_call_target="tpu_custom_call", output_to_operand_aliasing={{0}: (5, {}), {1}: (6, {})} | custom-call | flops 805306368 | bytes 6291456 | tf_op jit(solution)/shard_map/pallas_call | solution.py:188
  13.0 86.0 %all_to_all.20.query_ref.key_ref.grad_ref = bf16[32,768,128]{2,1,0:T(8,128)(2,1)} all-to-all(bf16[32,768,128]{2,1,0:T(8,128)(2,1)} %get-tuple-element.26), channel_id=1, replica_groups=mesh['clip'=4,'ctx'=32] {'ctx'}, dimensions={0} | all-to-all | bytes 12582912 | tf_op jit(solution)/shard_map/all_to_all | solution.py:511
  99.0 0.0 copy-start.6
  99.0 4.2 %all-to-all-start.1 = ((bf16[32,368,128]{2,1,0:T(8,128)(2,1)}), bf16[32,368,128]{2,1,0:T(8,128)(2,1)S(1)}, u32[]{:S(2)}, u32[]{:S(2)}) async-start(bf16[32,368,128]{2,1,0:T(8,128)(2,1)} %get-tuple-element.28), calls=%async_computation.1 | async-start | bytes 6029312 | tf_op jit(solution)/shard_map/all_to_all | solution.py:511
  103.2 0.0 copy-done.6
  103.2 0.1 copy.17
  103.3 0.7 reshape.15.pattern
  104.0 28.9 %shard_map.122 = (bf16[64,1024,128]{2,1,0:T(8,128)(2,1)}, bf16[64,128,128]{2,1,0:T(8,128)(2,1)}, bf16[32,368,128]{2,1,0:T(8,128)(2,1)}) custom-call(s32[512]{0:T(512)} %reshape.15.pattern, s32[64]{0:T(128)} %live.3, s32[64]{0:T(128)} %select_reduce_fusion.order, bf16[32,768,128]{2,1,0:T(8,128)(2,1)} %all_to_all.20.query_ref.key_ref.grad_ref, ...), custom_call_target="tpu_custom_call" | custom-call | flops 4294967296 | bytes 16777216 | tf_op jit(solution)/shard_map/pallas_call | solution.py:404
  132.9 13.3 %all-to-all-done.1.value_ref.terms_ref = bf16[32,368,128]{2,1,0:T(8,128)(2,1)S(1)} async-done(((bf16[32,368,128]{2,1,0:T(8,128)(2,1)}), bf16[32,368,128]{2,1,0:T(8,128)(2,1)S(1)}, u32[]{:S(2)}, u32[]{:S(2)}) %all-to-all-start.1) | async-done | bytes 3014688 | tf_op jit(solution)/shard_map/all_to_all | solution.py:511
  146.2 1.7 copy-done.4
  147.9 2.5 shard_map.124
  150.5 5.6 %all-to-all-start.2 = ((bf16[32,368,128]{2,1,0:T(8,128)(2,1)}), bf16[32,368,128]{2,1,0:T(8,128)(2,1)S(1)}, u32[]{:S(2)}, u32[]{:S(2)}) async-start(bf16[32,368,128]{2,1,0:T(8,128)(2,1)} %shard_map.124), calls=%async_computation.2 | async-start | bytes 6029312 | tf_op jit(solution)/shard_map/all_to_all | solution.py:511
  156.0 33.2 %shard_map.123 = bf16[32,512,128]{2,1,0:T(8,128)(2,1)} custom-call(s32[512]{0:T(512)} %reshape.15.pattern, s32[64]{0:T(128)} %live.3, s32[64]{0:T(128)} %select_reduce_fusion.order, bf16[32,768,128]{2,1,0:T(8,128)(2,1)} %all_to_all.20.query_ref.key_ref.grad_ref, bf16[32,768,128]{2,1,0:T(8,128)(2,1)} %all_to_all.20.query_ref.key_ref.grad_ref, ...), custom_call_target="tpu_custom_call" | custom-call | flops 6442450944 | bytes 33554432 | tf_op jit(solution)/shard_map/pallas_call | solution.py:485
  189.2 7.7 %all-to-all-done.2.last_ref = bf16[32,368,128]{2,1,0:T(8,128)(2,1)S(1)} async-done(((bf16[32,368,128]{2,1,0:T(8,128)(2,1)}), bf16[32,368,128]{2,1,0:T(8,128)(2,1)S(1)}, u32[]{:S(2)}, u32[]{:S(2)}) %all-to-all-start.2) | async-done | bytes 3014688 | tf_op jit(solution)/shard_map/all_to_all | solution.py:511
  197.0 53.8 %all_to_all.21.pair_ref = bf16[32,512,128]{2,1,0:T(8,128)(2,1)} all-to-all(bf16[32,512,128]{2,1,0:T(8,128)(2,1)} %shard_map.123), channel_id=1, replica_groups=mesh['clip'=4,'ctx'=32] {'ctx'}, dimensions={0} | all-to-all | bytes 8388608 | tf_op jit(solution)/shard_map/all_to_all | solution.py:511
  250.8 0.0 copy-done.5
  250.8 7.5 %shard_map.125 = (bf16[256,4096]{1,0:T(8,128)(2,1)}, bf16[256,4096]{1,0:T(8,128)(2,1)}, bf16[256,4096]{1,0:T(8,128)(2,1)}, f32[3,384,384]{2,1,0:T(8,128)}) custom-call(bf16[32,512,128]{2,1,0:T(8,128)(2,1)} %all_to_all.21.pair_ref, bf16[32,368,128]{2,1,0:T(8,128)(2,1)} %copy-done.5), custom_call_target="tpu_custom_call" | custom-call | bytes 12582912 | tf_op jit(solution)/shard_map/pallas_call | solution.py:307
  (2 shorter events, 0.0 us)
Async XLA Ops:
  0.6 8.9 %copy-start.2 = (bf16[2,128,384]{2,1,0:T(8,128)(2,1)S(1)}, bf16[2,128,384]{2,1,0:T(8,128)(2,1)}, u32[]{:S(2)}) copy-start(bf16[2,128,384]{2,1,0:T(8,128)(2,1)} %near_ref.1) | copy-start | bytes 589828
  0.6 8.0 %copy-start.7 = (s32[64]{0:T(128)S(1)}, s32[64]{0:T(128)}, u32[]{:S(2)}) copy-start(s32[64]{0:T(128)} %live.3) | copy-start | bytes 772
  0.7 8.9 %copy-start = (bf16[4096,384]{1,0:T(8,128)(2,1)S(1)}, bf16[4096,384]{1,0:T(8,128)(2,1)}, u32[]{:S(2)}) copy-start(bf16[4096,384]{1,0:T(8,128)(2,1)} %head_weight_ref.1) | copy-start | bytes 9437188
  0.7 8.9 %copy-start.1 = (bf16[3,384,384]{2,1,0:T(8,128)(2,1)S(1)}, bf16[3,384,384]{2,1,0:T(8,128)(2,1)}, u32[]{:S(2)}) copy-start(bf16[3,384,384]{2,1,0:T(8,128)(2,1)} %tap_weight_ref.1) | copy-start | bytes 2654212
  0.7 8.9 %copy-start.3 = (bf16[2,128,384]{2,1,0:T(8,128)(2,1)S(1)}, bf16[2,128,384]{2,1,0:T(8,128)(2,1)}, u32[]{:S(2)}) copy-start(bf16[2,128,384]{2,1,0:T(8,128)(2,1)} %feature_ref.1) | copy-start | bytes 589828
  0.7 8.8 %collective-permute-start = (bf16[2,128,384]{2,1,0:T(8,128)(2,1)}, bf16[2,128,384]{2,1,0:T(8,128)(2,1)S(1)}, u32[]{:S(2)}, u32[]{:S(2)}) collective-permute-start(bf16[2,128,384]{2,1,0:T(8,128)(2,1)} %near_ref.1), channel_id=1, source_target_pairs={{1,0},{2,1},{3,2},{4,3},{5,4},{6,5},{7,6},{8,7},{9,8},{10,9},{11,1... | collective-permute-start | bytes 589832 | tf_op jit(solution)/shard_map/ppermute | solution.py:522
  99.0 4.2 %copy-start.6 = (s32[64,8]{0,1:T(8,128)S(1)}, s32[64,8]{0,1:T(8,128)}, u32[]{:S(2)}) copy-start(s32[64,8]{0,1:T(8,128)} %param.16) | copy-start | bytes 6148
  99.0 47.2 %all-to-all-start.1 = ((bf16[32,368,128]{2,1,0:T(8,128)(2,1)}), bf16[32,368,128]{2,1,0:T(8,128)(2,1)S(1)}, u32[]{:S(2)}, u32[]{:S(2)}) async-start(bf16[32,368,128]{2,1,0:T(8,128)(2,1)} %get-tuple-element.28), calls=%async_computation.1 | async-start | bytes 6029312 | tf_op jit(solution)/shard_map/all_to_all | solution.py:511
  146.2 1.7 copy-start.4
  150.5 46.5 %all-to-all-start.2 = ((bf16[32,368,128]{2,1,0:T(8,128)(2,1)}), bf16[32,368,128]{2,1,0:T(8,128)(2,1)S(1)}, u32[]{:S(2)}, u32[]{:S(2)}) async-start(bf16[32,368,128]{2,1,0:T(8,128)(2,1)} %shard_map.124), calls=%async_computation.2 | async-start | bytes 6029312 | tf_op jit(solution)/shard_map/all_to_all | solution.py:511
  197.0 53.8 %copy-start.5 = (bf16[32,368,128]{2,1,0:T(8,128)(2,1)}, bf16[32,368,128]{2,1,0:T(8,128)(2,1)S(1)}, u32[]{:S(2)}) copy-start(bf16[32,368,128]{2,1,0:T(8,128)(2,1)S(1)} %all-to-all-done.2.last_ref) | copy-start | bytes 9043972

commit v2 on v1

--- a/solution.py
+++ b/solution.py
@@ -51,48 +51,27 @@
     return ref.at[:, pl.ds(head * DH, DH)]
 
 
-def relay(stages):
-    for arrivals, _ in stages:
-        for copy in arrivals:
-            copy.start()
-    for arrivals, departures in stages:
-        for copy in arrivals:
-            copy.wait()
-        for copy in departures:
-            copy.start()
-    for _, departures in stages:
-        for copy in departures:
-            copy.wait()
-
-
 def pack_kernel(query_ref, key_ref, value_ref, triple_ref, last_ref, held_ref, in_sems, out_sems):
     rows = query_ref.shape[0]
-    stages = []
-    for first in range(0, held_ref.shape[0], PACKED):
-        heads = pl.ds(first, PACKED)
-        arrivals = [
-            pltpu.make_async_copy(
-                columns_of(ref, head),
-                held_ref.at[head, pl.ds(place * rows, rows), :],
-                in_sems.at[place, head],
-            )
-            for head in range(first, first + PACKED)
-            for place, ref in enumerate((query_ref, key_ref, value_ref))
-        ]
-        departures = [
-            pltpu.make_async_copy(
-                held_ref.at[heads, pl.ds(0, 2 * rows), :],
-                triple_ref.at[heads, pl.ds(0, 2 * rows), :],
-                out_sems.at[0, first // PACKED],
-            ),
-            pltpu.make_async_copy(
-                held_ref.at[heads, pl.ds(2 * rows, rows), :],
-                last_ref.at[heads, pl.ds(0, rows), :],
-                out_sems.at[1, first // PACKED],
-            ),
-        ]
-        stages.append((arrivals, departures))
-    relay(stages)
+    arrivals = [
+        pltpu.make_async_copy(ref, held_ref.at[place], in_sems.at[place])
+        for place, ref in enumerate((query_ref, key_ref, value_ref))
+    ]
+    for copy in arrivals:
+        copy.start()
+    departures = []
+    for place, arrival in enumerate(arrivals):
+        arrival.wait()
+        for head in range(triple_ref.shape[0]):
+            source = held_ref.at[place, :, pl.ds(head * DH, DH)]
+            if place < 2:
+                target = triple_ref.at[head, pl.ds(place * rows, rows), :]
+            else:
+                target = last_ref.at[head, pl.ds(0, rows), :]
+            departures.append(pltpu.make_async_copy(source, target, out_sems.at[place, head]))
+            departures[-1].start()
+    for copy in departures:
+        copy.wait()
 
 
 def pack(queries, keys, values, held):
@@ -107,9 +86,9 @@
             pltpu.HBM((heads, rows + held, DH), BF16),
         ],
         scratch_shapes=[
-            pltpu.VMEM((heads, 3 * rows, DH), BF16),
+            pltpu.VMEM((3, rows, width), BF16),
+            pltpu.SemaphoreType.DMA((3,)),
             pltpu.SemaphoreType.DMA((3, heads)),
-            pltpu.SemaphoreType.DMA((2, heads // PACKED)),
         ],
         compiler_params=pltpu.CompilerParams(vmem_limit_bytes=SMALL_LIMIT),
         cost_estimate=pl.CostEstimate(flops=0, bytes_accessed=12 * rows * width, transcendentals=0),
@@ -206,15 +185,12 @@
     )(feat_grad, incoming, features, conv_weight, head_weight, in_hbm(triple), in_hbm(last))
 
 
-def share_sum_kernel(terms_ref, into_ref, out_ref, terms, total, in_sem, out_sems):
+def share_sum_kernel(terms_ref, into_ref, out_ref, total, sems):
     held = total.shape[0]
     rows = out_ref.shape[1] - held
-    arrival = pltpu.make_async_copy(terms_ref.at[:, pl.ds(rows, held), :], terms, in_sem)
-    arrival.start()
-    arrival.wait()
-    total[...] = jnp.sum(terms[...].astype(F32), axis=0).astype(BF16)
+    total[...] = jnp.sum(terms_ref[:, rows:, :].astype(F32), axis=0).astype(BF16)
     copies = [
-        pltpu.make_async_copy(total, out_ref.at[device, pl.ds(rows, held), :], out_sems.at[device])
+        pltpu.make_async_copy(total, out_ref.at[device, pl.ds(rows, held), :], sems.at[device])
         for device in range(out_ref.shape[0])
     ]
     for copy in copies:
@@ -227,66 +203,40 @@
     devices = terms.shape[0]
     return pl.pallas_call(
         share_sum_kernel,
-        in_specs=[HBM_SPEC] * 2,
+        in_specs=[VMEM_SPEC, HBM_SPEC],
         out_specs=HBM_SPEC,
         out_shape=pltpu.HBM(into.shape, into.dtype),
         scratch_shapes=[
-            pltpu.VMEM((devices, held, DH), BF16),
             pltpu.VMEM((held, DH), BF16),
-            pltpu.SemaphoreType.DMA(()),
             pltpu.SemaphoreType.DMA((devices,)),
         ],
         input_output_aliases={1: 0},
         compiler_params=pltpu.CompilerParams(vmem_limit_bytes=SMALL_LIMIT),
-    )(in_hbm(terms), in_hbm(into))
+    )(terms, in_hbm(into))
 
 
 def unpack_kernel(factor, pair_ref, last_ref, *refs):
-    *out_refs, tap_out_ref, held_ref, taps_ref, scaled_ref, in_sems, out_sems, tap_sems, done_sem = refs
+    *out_refs, tap_out_ref, held_ref, taps_ref, scaled_ref, in_sems, out_sems, done_sem = refs
     heads, rows = held_ref.shape[0], out_refs[0].shape[0]
     share = last_ref.shape[1] - rows
-    tap_copies = [
-        pltpu.make_async_copy(
-            last_ref.at[device, pl.ds(rows, share), :],
-            taps_ref.at[pl.ds(device * share, share), :],
-            tap_sems.at[device],
-        )
-        for device in range(heads)
-    ]
-    stages = []
+    arrivals = []
     for first in range(0, heads, PACKED):
         group = pl.ds(first, PACKED)
-        places = [(pair_ref, 0, 2 * rows), (last_ref, 2 * rows, rows)]
-        arrivals = [
+        arrivals.append(
             pltpu.make_async_copy(
-                ref.at[group, pl.ds(0, length), :],
-                held_ref.at[group, pl.ds(start, length), :],
-                in_sems.at[place, first // PACKED],
+                pair_ref.at[group], held_ref.at[group], in_sems.at[first // PACKED]
             )
-            for place, (ref, start, length) in enumerate(places)
-        ]
-        departures = [
-            pltpu.make_async_copy(
-                held_ref.at[head, pl.ds(place * rows, rows), :],
-                columns_of(out_ref, head),
-                out_sems.at[place, head],
-            )
-            for head in range(first, first + PACKED)
-            for place, out_ref in enumerate(out_refs)
-        ]
-        stages.append((arrivals, departures))
-    for arrivals, _ in stages:
-        for copy in arrivals:
-            copy.start()
-    for copy in tap_copies:
-        copy.start()
-    for arrivals, departures in stages:
-        for copy in arrivals:
-            copy.wait()
-        for copy in departures:
-            copy.start()
-    for copy in tap_copies:
-        copy.wait()
+        )
+        arrivals[-1].start()
+    departures = []
+    for head in range(heads):
+        source = last_ref.at[head, pl.ds(0, rows), :]
+        departures.append(
+            pltpu.make_async_copy(source, columns_of(out_refs[2], head), out_sems.at[2, head])
+        )
+        departures[-1].start()
+    for head in range(heads):
+        taps_ref[head * share : (head + 1) * share, :] = last_ref[head, rows:, :]
     taps, channels, width = scaled_ref.shape
     row = 0
     for k in range(taps):
@@ -294,36 +244,44 @@
             terms = taps_ref[row : row + channels, :].astype(F32) * factor
             scaled_ref[k, :, first : first + DH] = terms
             row += channels
-    done = pltpu.make_async_copy(scaled_ref, tap_out_ref, done_sem)
-    done.start()
-    for _, departures in stages:
-        for copy in departures:
-            copy.wait()
-    done.wait()
+    departures.append(pltpu.make_async_copy(scaled_ref, tap_out_ref, done_sem))
+    departures[-1].start()
+    for place, arrival in enumerate(arrivals):
+        arrival.wait()
+        for head in range(place * PACKED, (place + 1) * PACKED):
+            for part in range(2):
+                source = held_ref.at[head, pl.ds(part * rows, rows), :]
+                departures.append(
+                    pltpu.make_async_copy(
+                        source, columns_of(out_refs[part], head), out_sems.at[part, head]
+                    )
+                )
+                departures[-1].start()
+    for copy in departures:
+        copy.wait()
 
 
 def unpack(pair, last, tap_shape, factor):
     heads, rows = pair.shape[0], pair.shape[1] // 2
     return pl.pallas_call(
         functools.partial(unpack_kernel, factor),
-        in_specs=[HBM_SPEC] * 2,
+        in_specs=[HBM_SPEC, VMEM_SPEC],
         out_specs=[HBM_SPEC] * 4,
         out_shape=[jax.ShapeDtypeStruct((rows, heads * DH), last.dtype)] * 3
         + [jax.ShapeDtypeStruct(tap_shape, F32)],
         scratch_shapes=[
-            pltpu.VMEM((heads, 3 * rows, DH), last.dtype),
+            pltpu.VMEM((heads, 2 * rows, DH), last.dtype),
             pltpu.VMEM((heads * (last.shape[1] - rows), DH), last.dtype),
             pltpu.VMEM(tap_shape, F32),
-            pltpu.SemaphoreType.DMA((2, heads // PACKED)),
+            pltpu.SemaphoreType.DMA((heads // PACKED,)),
             pltpu.SemaphoreType.DMA((3, heads)),
-            pltpu.SemaphoreType.DMA((heads,)),
             pltpu.SemaphoreType.DMA(()),
         ],
         compiler_params=pltpu.CompilerParams(vmem_limit_bytes=SMALL_LIMIT),
         cost_estimate=pl.CostEstimate(
             flops=0, bytes_accessed=12 * rows * heads * DH, transcendentals=0
         ),
-    )(in_hbm(pair), in_hbm(last))
+    )(in_hbm(pair), last)
 
 
 def clear(total_ref):

time: 261 us -> 257 us (0.985)
  Pallas kernels: 82 us -> 78.2 us
where the time goes in v2:
time: 257 us; the launch traced here: 255 us
  blocking collectives  140 us (54%)
  Pallas kernels  78.2 us (30%)
  waiting for transfers between devices  22.2 us (9%)
  starting transfers between devices  11.3 us (4%)
    all_to_all x2, blocking collectives, exchange(): lax.all_to_all(blocks, 'ctx', split_axis=0, concat_axis=0, tiled=True)  140 us
    pallas_call x1, Pallas kernels, grads_of(): pl.pallas_call(functools.partial(grads_kernel, listed), grid_spec=pltpu.P...  32.9 us
    pallas_call x1, Pallas kernels, probs_of(): pl.pallas_call(functools.partial(probs_kernel, listed), grid_spec=pltpu.P...  28.8 us
    all_to_all x2, waiting for transfers between devices, exchange(): lax.all_to_all(blocks, 'ctx', split_axis=0, concat_axis=0, tiled=True)  21.5 us
    all_to_all x2, starting transfers between devices, exchange(): lax.all_to_all(blocks, 'ctx', split_axis=0, concat_axis=0, tiled=True)  9.74 us
    pallas_call x1, Pallas kernels, unpack(): pl.pallas_call(functools.partial(unpack_kernel, factor), in_specs=[HBM_SP...  5.83 us
    pallas_call x1, Pallas kernels, pack(): pl.pallas_call(pack_kernel, in_specs=[HBM_SPEC] * 3, out_specs=[HBM_SPEC]...  5.73 us
  transfers between devices with their start and end apart: 3, of which 3 were waited for; matrix products, arithmetic and copies ran while one was open for 1% of the time, Pallas kernels for 26%

profile of v2, /device:TPU:0, one launch (start us, length us, event | category | flops | bytes accessed | tf_op | source)
XLA Modules:
  0.0 254.6 jit_solution(6064360325836948434)
XLA Ops:
  0.6 0.0 copy-start.3
  0.6 0.0 copy-start.6
  0.7 0.0 copy-start.1
  0.7 0.0 copy-start.2
  0.7 0.0 copy-start.4
  0.7 1.6 collective-permute-start
  2.2 5.7 %shard_map.120 = (bf16[32,768,128]{2,1,0:T(8,128)(2,1)}, bf16[32,368,128]{2,1,0:T(8,128)(2,1)}) custom-call(bf16[256,4096]{1,0:T(8,128)(2,1)} %query_ref.1, bf16[256,4096]{1,0:T(8,128)(2,1)} %key_ref.1, bf16[256,4096]{1,0:T(8,128)(2,1)} %value_ref.1), custom_call_target="tpu_custom_call" | custom-call | bytes 12582912 | tf_op jit(solution)/shard_map/pallas_call | solution.py:80
  8.0 0.0 copy-done.6
  8.0 0.2 convert_reduce_fusion
  8.2 0.6 select_reduce_fusion.order
  8.8 0.7 collective-permute-done.next_ref
  9.5 0.0 copy-done.3
  9.5 0.0 copy-done.1
  9.5 0.0 copy-done.2
  9.5 0.0 copy-done.4
  9.6 3.5 %shard_map.121 = (bf16[32,768,128]{2,1,0:T(8,128)(2,1)}, bf16[32,368,128]{2,1,0:T(8,128)(2,1)}) custom-call(bf16[2,128,384]{2,1,0:T(8,128)(2,1)S(1)} %copy-done.3, bf16[2,128,384]{2,1,0:T(8,128)(2,1)S(1)} %collective-permute-done.next_ref, bf16[2,128,384]{2,1,0:T(8,128)(2,1)S(1)} %copy-done.4, ...), custom_call_target="tpu_custom_call", output_to_operand_aliasing={{0}: (5, {}), {1}: (6, {})} | custom-call | flops 805306368 | bytes 6291456 | tf_op jit(solution)/shard_map/pallas_call | solution.py:167
  13.0 86.0 %all_to_all.20.query_ref.key_ref.grad_ref = bf16[32,768,128]{2,1,0:T(8,128)(2,1)} all-to-all(bf16[32,768,128]{2,1,0:T(8,128)(2,1)} %get-tuple-element.26), channel_id=1, replica_groups=mesh['clip'=4,'ctx'=32] {'ctx'}, dimensions={0} | all-to-all | bytes 12582912 | tf_op jit(solution)/shard_map/all_to_all | solution.py:469
  99.1 0.0 copy-start.5
  99.1 4.2 %all-to-all-start.1 = ((bf16[32,368,128]{2,1,0:T(8,128)(2,1)}), bf16[32,368,128]{2,1,0:T(8,128)(2,1)S(1)}, u32[]{:S(2)}, u32[]{:S(2)}) async-start(bf16[32,368,128]{2,1,0:T(8,128)(2,1)} %get-tuple-element.28), calls=%async_computation.1 | async-start | bytes 6029312 | tf_op jit(solution)/shard_map/all_to_all | solution.py:469
  103.3 0.0 copy-done.5
  103.3 0.1 copy.17
  103.4 0.7 reshape.15.pattern
  104.0 28.8 %shard_map.122 = (bf16[64,1024,128]{2,1,0:T(8,128)(2,1)}, bf16[64,128,128]{2,1,0:T(8,128)(2,1)}, bf16[32,368,128]{2,1,0:T(8,128)(2,1)}) custom-call(s32[512]{0:T(512)} %reshape.15.pattern, s32[64]{0:T(128)} %live.3, s32[64]{0:T(128)} %select_reduce_fusion.order, bf16[32,768,128]{2,1,0:T(8,128)(2,1)} %all_to_all.20.query_ref.key_ref.grad_ref, ...), custom_call_target="tpu_custom_call" | custom-call | flops 4294967296 | bytes 16777216 | tf_op jit(solution)/shard_map/pallas_call | solution.py:362
  132.8 13.4 %all-to-all-done.1.value_ref.terms_ref = bf16[32,368,128]{2,1,0:T(8,128)(2,1)S(1)} async-done(((bf16[32,368,128]{2,1,0:T(8,128)(2,1)}), bf16[32,368,128]{2,1,0:T(8,128)(2,1)S(1)}, u32[]{:S(2)}, u32[]{:S(2)}) %all-to-all-start.1) | async-done | bytes 3014688 | tf_op jit(solution)/shard_map/all_to_all | solution.py:469
  146.2 0.0 copy-start
  146.2 1.5 shard_map.124
  147.8 0.5 copy-done
  148.2 5.5 %all-to-all-start.2 = ((bf16[32,368,128]{2,1,0:T(8,128)(2,1)}), bf16[32,368,128]{2,1,0:T(8,128)(2,1)S(1)}, u32[]{:S(2)}, u32[]{:S(2)}) async-start(bf16[32,368,128]{2,1,0:T(8,128)(2,1)} %shard_map.124), calls=%async_computation.2 | async-start | bytes 6029312 | tf_op jit(solution)/shard_map/all_to_all | solution.py:469
  153.8 32.9 %shard_map.123 = bf16[32,512,128]{2,1,0:T(8,128)(2,1)} custom-call(s32[512]{0:T(512)} %reshape.15.pattern, s32[64]{0:T(128)} %live.3, s32[64]{0:T(128)} %select_reduce_fusion.order, bf16[32,768,128]{2,1,0:T(8,128)(2,1)} %all_to_all.20.query_ref.key_ref.grad_ref, bf16[32,768,128]{2,1,0:T(8,128)(2,1)} %all_to_all.20.query_ref.key_ref.grad_ref, ...), custom_call_target="tpu_custom_call" | custom-call | flops 6442450944 | bytes 33554432 | tf_op jit(solution)/shard_map/pallas_call | solution.py:443
  186.7 8.0 %all-to-all-done.2.last_ref = bf16[32,368,128]{2,1,0:T(8,128)(2,1)S(1)} async-done(((bf16[32,368,128]{2,1,0:T(8,128)(2,1)}), bf16[32,368,128]{2,1,0:T(8,128)(2,1)S(1)}, u32[]{:S(2)}, u32[]{:S(2)}) %all-to-all-start.2) | async-done | bytes 3014688 | tf_op jit(solution)/shard_map/all_to_all | solution.py:469
  194.7 53.8 %all_to_all.21.pair_ref = bf16[32,512,128]{2,1,0:T(8,128)(2,1)} all-to-all(bf16[32,512,128]{2,1,0:T(8,128)(2,1)} %shard_map.123), channel_id=1, replica_groups=mesh['clip'=4,'ctx'=32] {'ctx'}, dimensions={0} | all-to-all | bytes 8388608 | tf_op jit(solution)/shard_map/all_to_all | solution.py:469
  248.6 5.8 %shard_map.125 = (bf16[256,4096]{1,0:T(8,128)(2,1)}, bf16[256,4096]{1,0:T(8,128)(2,1)}, bf16[256,4096]{1,0:T(8,128)(2,1)}, f32[3,384,384]{2,1,0:T(8,128)}) custom-call(bf16[32,512,128]{2,1,0:T(8,128)(2,1)} %all_to_all.21.pair_ref, bf16[32,368,128]{2,1,0:T(8,128)(2,1)S(1)} %all-to-all-done.2.last_ref), custom_call_target="tpu_custom_call" | custom-call | bytes 12582912 | tf_op jit(solution)/shard_map/pallas_call | solution.py:266
Async XLA Ops:
  0.6 8.9 %copy-start.3 = (bf16[2,128,384]{2,1,0:T(8,128)(2,1)S(1)}, bf16[2,128,384]{2,1,0:T(8,128)(2,1)}, u32[]{:S(2)}) copy-start(bf16[2,128,384]{2,1,0:T(8,128)(2,1)} %near_ref.1) | copy-start | bytes 589828
  0.6 7.3 %copy-start.6 = (s32[64]{0:T(128)S(1)}, s32[64]{0:T(128)}, u32[]{:S(2)}) copy-start(s32[64]{0:T(128)} %live.3) | copy-start | bytes 772
  0.7 8.9 %copy-start.1 = (bf16[4096,384]{1,0:T(8,128)(2,1)S(1)}, bf16[4096,384]{1,0:T(8,128)(2,1)}, u32[]{:S(2)}) copy-start(bf16[4096,384]{1,0:T(8,128)(2,1)} %head_weight_ref.1) | copy-start | bytes 9437188
  0.7 8.9 %copy-start.2 = (bf16[3,384,384]{2,1,0:T(8,128)(2,1)S(1)}, bf16[3,384,384]{2,1,0:T(8,128)(2,1)}, u32[]{:S(2)}) copy-start(bf16[3,384,384]{2,1,0:T(8,128)(2,1)} %tap_weight_ref.1) | copy-start | bytes 2654212
  0.7 8.9 %copy-start.4 = (bf16[2,128,384]{2,1,0:T(8,128)(2,1)S(1)}, bf16[2,128,384]{2,1,0:T(8,128)(2,1)}, u32[]{:S(2)}) copy-start(bf16[2,128,384]{2,1,0:T(8,128)(2,1)} %feature_ref.1) | copy-start | bytes 589828
  0.7 8.8 %collective-permute-start = (bf16[2,128,384]{2,1,0:T(8,128)(2,1)}, bf16[2,128,384]{2,1,0:T(8,128)(2,1)S(1)}, u32[]{:S(2)}, u32[]{:S(2)}) collective-permute-start(bf16[2,128,384]{2,1,0:T(8,128)(2,1)} %near_ref.1), channel_id=1, source_target_pairs={{1,0},{2,1},{3,2},{4,3},{5,4},{6,5},{7,6},{8,7},{9,8},{10,9},{11,1... | collective-permute-start | bytes 589832 | tf_op jit(solution)/shard_map/ppermute | solution.py:480
  99.1 4.2 %copy-start.5 = (s32[64,8]{0,1:T(8,128)S(1)}, s32[64,8]{0,1:T(8,128)}, u32[]{:S(2)}) copy-start(s32[64,8]{0,1:T(8,128)} %param.16) | copy-start | bytes 6148
  99.1 47.2 %all-to-all-start.1 = ((bf16[32,368,128]{2,1,0:T(8,128)(2,1)}), bf16[32,368,128]{2,1,0:T(8,128)(2,1)S(1)}, u32[]{:S(2)}, u32[]{:S(2)}) async-start(bf16[32,368,128]{2,1,0:T(8,128)(2,1)} %get-tuple-element.28), calls=%async_computation.1 | async-start | bytes 6029312 | tf_op jit(solution)/shard_map/all_to_all | solution.py:469
  146.2 2.0 copy-start
  148.2 46.5 %all-to-all-start.2 = ((bf16[32,368,128]{2,1,0:T(8,128)(2,1)}), bf16[32,368,128]{2,1,0:T(8,128)(2,1)S(1)}, u32[]{:S(2)}, u32[]{:S(2)}) async-start(bf16[32,368,128]{2,1,0:T(8,128)(2,1)} %shard_map.124), calls=%async_computation.2 | async-start | bytes 6029312 | tf_op jit(solution)/shard_map/all_to_all | solution.py:469
